TPU v7x, 256 devices: a whole 4x4x8 slice. The times are simulated.
256 devices in a mesh: replica: 8 (over z_lo, core), fsdp: 32 (over y, x, z_hi).
Axes of the slice: x: 4, y: 4, z: 8 (z_hi: 2, z_lo: 4; z = z_hi * 4 + z_lo), core: 2. Of those that a mesh axis runs over, the one named last changes fastest.
Arguments:
- tok_inputs: bfloat16 [8, 8192, 256], P('replica', 'fsdp'), may hold values from -6 to 6
- tok_grads: bfloat16 [8, 8192, 14336], P('replica', 'fsdp'), may hold values from -0.0625 to 0.0625
- inner_params: float32 [8, 256, 14336], P('replica', 'fsdp'), may hold values from -4 to 4
- adam_first: float32 [8, 256, 14336], P('replica', 'fsdp'), may hold values from -3 to 3
- adam_second: float32 [8, 256, 14336], P('replica', 'fsdp'), may hold values from 0.05 to 1
- global_params: float32 [256, 14336], P('fsdp'), may hold values from -4 to 4
- outer_momentum: float32 [256, 14336], P('fsdp'), may hold values from -3 to 3
Outputs:
- first_moment: float32 [8, 256, 14336], P('replica', 'fsdp')
- second_moment: float32 [8, 256, 14336], P('replica', 'fsdp')
- global_next: float32 [256, 14336], P('fsdp')
- momentum_next: float32 [256, 14336], P('fsdp')
All inputs are finite; a program needn't handle non-finite values.
Results may differ from a plain program's by a relative error of at most 0.0003.
Values may be sent and summed in bfloat16 or wider, within the bound.
A program may use at most 128 MiB of HBM per device.

v0:
```python
import jax
import jax.numpy as jnp
from jax import lax
from jax.sharding import PartitionSpec as P

beta_first = 0.9
beta_second = 0.95
inner_rate = 0.1
outer_rate = 0.7
momentum_decay = 0.9
epsilon = 1e-08
first_correction = 1.0 - 0.9**40
second_correction = 1.0 - 0.95**40


def outer_step(average, momentum, weights):
    momentum_next = momentum_decay * momentum + average
    global_next = weights - outer_rate * (average + momentum_decay * momentum_next)
    return (global_next, momentum_next)


def shards(
    tok_inputs, tok_grads, inner_params, adam_first, adam_second, global_params, outer_momentum
):
    features = tok_inputs[0]
    upstream = tok_grads[0]
    gradient = lax.psum_scatter(
        lax.dot_general(
            features, upstream, (((0,), (0,)), ((), ())), preferred_element_type=jnp.float32
        ),
        "fsdp",
        scatter_dimension=0,
        tiled=True,
    )
    first_moment = beta_first * adam_first[0] + (1.0 - beta_first) * gradient
    second_moment = beta_second * adam_second[0] + (1.0 - beta_second) * gradient * gradient
    update = (
        first_moment / first_correction / (jnp.sqrt(second_moment / second_correction) + epsilon)
    )
    inner_next = inner_params[0] - inner_rate * update
    pseudo = global_params - inner_next
    replica_count = lax.axis_size("replica")
    total = lax.psum(pseudo, "replica")
    global_next, momentum_next = outer_step(total / replica_count, outer_momentum, global_params)
    return (first_moment[None], second_moment[None], global_next, momentum_next)


def solution(mesh):
    placed = (
        P("replica", "fsdp", None),
        P("replica", "fsdp", None),
        P("replica", "fsdp", None),
        P("replica", "fsdp", None),
        P("replica", "fsdp", None),
        P("fsdp", None),
        P("fsdp", None),
    )
    return jax.shard_map(
        shards,
        mesh=mesh,
        in_specs=placed,
        out_specs=(
            P("replica", "fsdp", None),
            P("replica", "fsdp", None),
            P("fsdp", None),
            P("fsdp", None),
        ),
        check_vma=False,
    )
```

profile of v0, /device:TPU:1, one launch (start us, length us, event | category | flops | bytes accessed | tf_op | source)
XLA Modules:
  0.0 732.8 jit_solution(5455206877803160177)
XLA Ops:
  7.2 0.0 copy-start
  7.2 0.0 reduce-scatter.2.cloned.1.call-start
  7.2 0.8 copy-done
  8.1 10.4 %fusion = f32[256,14336]{1,0:T(8,128)} fusion(bf16[1,256,14336]{2,1,0:T(8,128)(2,1)} %param.8, bf16[1,256,256]{2,1,0:T(8,128)(2,1)S(1)} %copy-done), kind=kOutput, calls=%fused_computation | convolution fusion | flops 1879048192 | bytes 22151168 | tf_op jit(solution)/shard_map/dot_general | solution.py:28
  18.4 0.0 copy-start.1
  18.4 0.0 copy-start.2
  18.5 0.0 copy-start.3
  18.5 0.0 copy-start.4
  18.5 0.0 copy-start.5
  18.5 0.0 reduce-scatter.2.cloned.1.call-update
  18.5 0.0 all-reduce.2.cloned.1.call-start
  18.5 637.9 %reduce-scatter.2.cloned.1.call-done = f32[8,14336]{1,0:T(8,128)} async-done(((f32[256,14336]{1,0:T(8,128)}), f32[8,14336]{1,0:T(8,128)}) %reduce-scatter.2.cloned.1.call-update) | async-done | bytes 458768 | tf_op jit(solution)/shard_map/reduce_scatter | solution.py:27
  656.5 0.0 copy-done.1
  656.5 0.0 copy-done.2
  656.5 0.0 copy-done.3
  656.5 0.0 copy-done.4
  656.5 2.3 fusion.3
  658.8 0.0 all-reduce.2.cloned.1.call-update
  658.8 65.2 %all-reduce.2.cloned.1.call-done = f32[8,14336]{1,0:T(8,128)} async-done(((f32[8,14336]{1,0:T(8,128)}), f32[8,14336]{1,0:T(8,128)}) %all-reduce.2.cloned.1.call-update) | async-done | bytes 458768 | tf_op jit(solution)/shard_map/psum | solution.py:43
  723.9 0.0 copy-done.5
  723.9 2.1 multiply_subtract_fusion
Async XLA Ops:
  7.2 0.9 copy-start
  7.2 649.3 %reduce-scatter.2.cloned.1.call-start = ((), (), s32[]{:S(2)}) async-start(), calls=%async_computation.1 | async-start | bytes 15138816 | tf_op jit(solution)/shard_map/reduce_scatter | solution.py:27
  18.4 638.0 %copy-start.1 = (f32[8,14336]{1,0:T(8,128)S(1)}, f32[8,14336]{1,0:T(8,128)}, u32[]{:S(2)}) copy-start(f32[8,14336]{1,0:T(8,128)} %param.12) | copy-start | bytes 1376260
  18.4 638.0 %copy-start.2 = (f32[1,8,14336]{2,1,0:T(8,128)S(1)}, f32[1,8,14336]{2,1,0:T(8,128)}, u32[]{:S(2)}) copy-start(f32[1,8,14336]{2,1,0:T(8,128)} %param.9) | copy-start | bytes 1376260
  18.5 638.0 %copy-start.3 = (f32[1,8,14336]{2,1,0:T(8,128)S(1)}, f32[1,8,14336]{2,1,0:T(8,128)}, u32[]{:S(2)}) copy-start(f32[1,8,14336]{2,1,0:T(8,128)} %param.10) | copy-start | bytes 1376260
  18.5 638.0 %copy-start.4 = (f32[1,8,14336]{2,1,0:T(8,128)S(1)}, f32[1,8,14336]{2,1,0:T(8,128)}, u32[]{:S(2)}) copy-start(f32[1,8,14336]{2,1,0:T(8,128)} %param.11) | copy-start | bytes 1376260
  18.5 705.5 %copy-start.5 = (f32[8,14336]{1,0:T(8,128)S(1)}, f32[8,14336]{1,0:T(8,128)}, u32[]{:S(2)}) copy-start(f32[8,14336]{1,0:T(8,128)} %param.13) | copy-start | bytes 1376260
  18.5 705.4 %all-reduce.2.cloned.1.call-start = ((), (), s32[]{:S(2)}) async-start(), calls=%async_computation.2 | async-start | bytes 917504 | tf_op jit(solution)/shard_map/psum | solution.py:43
Sparse Core Ops, SparseCore 0:
  18.6 637.8 reduce-scatter.1
  659.7 64.2 all-reduce.1
where the time goes:
time: 735 us; the launch traced here: 733 us
  waiting for transfers between devices  703 us (96%)
  between operations  14.1 us (2%)
  matrix products  10.4 us (1%)
    reduce_scatter x1, waiting for transfers between devices, shards(): lax.psum_scatter(lax.dot_general(features, upstream, (((0,), (0,)), ((),...  638 us
    psum x1, waiting for transfers between devices, shards(): total = lax.psum(pseudo, 'replica')  65.2 us
  transfers between devices with their start and end apart: 2, of which 2 were waited for; matrix products, arithmetic and copies ran while one was open for 0% of the time, Pallas kernels for 0%

commit v1 on v0

v1 whole, which is shorter than its diff:
```python
import functools
import jax
import jax.numpy as jnp
from jax import lax
from jax.experimental import pallas as pl
from jax.experimental.pallas import tpu as pltpu
from jax.sharding import PartitionSpec as P

beta_first = 0.9
beta_second = 0.95
inner_rate = 0.1
outer_rate = 0.7
momentum_decay = 0.9
epsilon = 1e-08
first_correction = 1.0 - 0.9**40
second_correction = 1.0 - 0.95**40

MESH = pl.DeviceIdType.MESH
SIDE = 4
WIDE = 1024
HALF = WIDE // 2
PIECE = WIDE // SIDE
POWER = 7
SCALES = (10, 8, 7)


def encode(value, stage):
    u = value * (2.0 ** SCALES[stage])
    u2 = u * u
    return (u2 * u2 * (u2 * u)).astype(jnp.bfloat16)


def decode_add(total, code, stage):
    y = code.astype(jnp.float32)
    size = jnp.exp2(jnp.log2(jnp.abs(y)) * (1.0 / POWER) - SCALES[stage])
    return jnp.where(y < 0, total - size, total + size)


def kernel(
    feat_ref, g_hbm, p_hbm, a1_hbm, a2_hbm, w_hbm, m_hbm,
    fm_ref, sm_ref, gn_ref, mn_ref,
    feat_t, g_ref, par, part, s1, r1, s2, r2, sz, rz, pse, mrecv, ssum, lrecv, tot,
    g_sem, par_sem, xy_send, xy_recv, z_send, z_recv, m_send, m_recv, l_send, l_recv, b_send, b_recv,
):
    ff = g_ref.shape[1]
    fh = ff // 2
    chunks = fh // WIDE
    rep = lax.axis_index("replica")
    fs = lax.axis_index("fsdp")
    q, k = rep // 2, rep % 2
    pos = (fs // 8, (fs // 2) % SIDE)
    zh = fs % 2
    zpeer = (rep, fs + 1 - 2 * zh)
    mate = (rep + 1 - 2 * k, fs)

    def ring(axis, step):
        y, x = pos
        if axis == 0:
            y = (y + step) % SIDE
        else:
            x = (x + step) % SIDE
        return (rep, y * 8 + x * 2 + zh)

    def start_col(c, h):
        return pl.multiple_of(h * fh + c * WIDE, WIDE)

    def g_copy(c, h):
        cols = pl.ds(start_col(c, h), WIDE)
        return pltpu.make_async_copy(g_hbm.at[:, cols], g_ref.at[:, cols], g_sem.at[c, h])

    par_copies = [
        pltpu.make_async_copy(src, par.at[i], par_sem.at[i])
        for i, src in enumerate((p_hbm, a1_hbm, a2_hbm, w_hbm, m_hbm))
    ]
    for h in range(2):
        g_copy(0, h).start()

    barrier = pltpu.get_barrier_semaphore()
    peers = [ring(a, s) for a in range(2) for s in (1, 3)] + [zpeer]
    peers += [((rep + d) % 8, fs) for d in range(1, 8)]
    for peer in peers:
        pl.semaphore_signal(barrier, inc=1, device_id=peer, device_id_type=MESH)

    @pl.loop(1, chunks)
    def _(c):
        for h in range(2):
            g_copy(c, h).start()

    for copy in par_copies:
        copy.start()

    feat_t[0] = feat_ref[...].astype(jnp.float32).T.astype(jnp.bfloat16)
    for y in range(SIDE):
        for x in range(SIDE):
            feat_t[1, pl.ds((x * SIDE + y) * 16, 16), :] = feat_t[0, pl.ds((y * SIDE + x) * 16, 16), :]

    def xy_copy(c, h, p, d, m):
        send, recv = ((s1, r1), (s2, r2))[p]
        slots = pl.ds(0, 2) if m == 0 else pl.ds(2, 1)
        return pltpu.make_async_remote_copy(
            src_ref=send.at[c, h, d, slots],
            dst_ref=recv.at[c, h, d, slots],
            send_sem=xy_send.at[c, ((h * 2 + p) * 2 + d) * 2 + m],
            recv_sem=xy_recv.at[c, ((h * 2 + p) * 2 + d) * 2 + m],
            device_id=ring((h + p) % 2, 1 if d == 0 else SIDE - 1),
            device_id_type=MESH,
        )

    def z_copy(c):
        return pltpu.make_async_remote_copy(
            src_ref=sz.at[c], dst_ref=rz.at[c], send_sem=z_send.at[c], recv_sem=z_recv.at[c],
            device_id=zpeer, device_id_type=MESH,
        )

    def m_copy(c):
        return pltpu.make_async_remote_copy(
            src_ref=pse.at[c, 1 - k], dst_ref=mrecv.at[c], send_sem=m_send.at[c], recv_sem=m_recv.at[c],
            device_id=mate, device_id_type=MESH,
        )

    def l_copy(c, d):
        to = (q + d) % SIDE
        return pltpu.make_async_remote_copy(
            src_ref=ssum.at[c, to], dst_ref=lrecv.at[c, d - 1],
            send_sem=l_send.at[c, d - 1], recv_sem=l_recv.at[c, d - 1],
            device_id=(to * 2 + k, fs), device_id_type=MESH,
        )

    def b_copy(c, d):
        return pltpu.make_async_remote_copy(
            src_ref=tot.at[c, 0], dst_ref=tot.at[c, d],
            send_sem=b_send.at[c, d - 1], recv_sem=b_recv.at[c, d - 1],
            device_id=((rep + d) % 8, fs), device_id_type=MESH,
        )

    def places(c, h, p):
        j = pos[(h + p) % 2]
        right = pl.ds(start_col(c, h), HALF)
        left = pl.ds(pl.multiple_of(start_col(c, h) + HALF, HALF), HALF)

        def at(dest, i, cols):
            dest = dest % SIDE
            return (dest, i, slice(None), cols) if p == 0 else (pos[h], dest, slice(None), cols)

        return j, right, left, at

    def over_blocks(p, body):
        if p == 0:
            pl.loop(0, SIDE)(body)
        else:
            body(0)

    def first_sends(c, h, p):
        send = (s1, s2)[p]
        j, right, left, at = places(c, h, p)

        def body(i):
            send[c, h, 0, 0, i] = encode(part[at(j + 2, i, right)], p)
            send[c, h, 0, 1, i] = encode(part[at(j + 1, i, left)], p)
            send[c, h, 1, 0, i] = encode(part[at(j + 2, i, left)], p)
            send[c, h, 1, 1, i] = encode(part[at(j + 3, i, right)], p)

        over_blocks(p, body)
        for d in range(2):
            xy_copy(c, h, p, d, 0).start()

    def second_sends(c, h, p):
        send, recv = ((s1, r1), (s2, r2))[p]
        j, right, left, at = places(c, h, p)
        for d in range(2):
            xy_copy(c, h, p, d, 0).wait_recv()

        def body(i):
            send[c, h, 0, 2, i] = encode(decode_add(part[at(j + 1, i, right)], recv[c, h, 0, 0, i], p), p)
            send[c, h, 1, 2, i] = encode(decode_add(part[at(j + 3, i, left)], recv[c, h, 1, 0, i], p), p)

        over_blocks(p, body)
        for d in range(2):
            xy_copy(c, h, p, d, 1).start()

    def collect(c, h, p):
        recv = (r1, r2)[p]
        j, right, left, at = places(c, h, p)
        for d in range(2):
            xy_copy(c, h, p, d, 1).wait_recv()

        def body(i):
            part[at(j, i, right)] = decode_add(
                decode_add(part[at(j, i, right)], recv[c, h, 0, 2, i], p), recv[c, h, 1, 1, i], p
            )
            part[at(j, i, left)] = decode_add(
                decode_add(part[at(j, i, left)], recv[c, h, 0, 1, i], p), recv[c, h, 1, 2, i], p
            )

        over_blocks(p, body)

    def multiply(c, h):
        g_copy(c, h).wait()

        @pl.loop(0, WIDE // 256)
        def _(t):
            cols = pl.ds(pl.multiple_of(start_col(c, h) + t * 256, 256), 256)
            part[:, :, :, cols] = jnp.dot(
                feat_t[h], g_ref[:, cols], preferred_element_type=jnp.float32
            ).reshape(SIDE, SIDE, 16, 256)

    def rows_of(h, whose, cols):
        return (pos[h], pos[1 - h], pl.ds(pl.multiple_of(whose * 8, 8), 8), cols)

    def stage0(c):
        for h in range(2):
            multiply(c, h)

            if h == 0:
                @pl.when(c == 0)
                def _():
                    pl.semaphore_wait(barrier, len(peers))

            first_sends(c, h, 0)

    def stage1(c):
        for h in range(2):
            second_sends(c, h, 0)

    def stage2(c):
        for h in range(2):
            collect(c, h, 0)
            first_sends(c, h, 1)

    def stage3(c):
        for h in range(2):
            second_sends(c, h, 1)

    def stage4(c):
        for h in range(2):
            collect(c, h, 1)

        @pl.loop(0, WIDE // HALF)
        def _(t):
            both = [
                part[rows_of(h, 1 - zh, pl.ds(pl.multiple_of(start_col(c, h) + t * HALF, HALF), HALF))]
                for h in range(2)
            ]
            sz[c, :, pl.ds(pl.multiple_of(t * HALF, HALF), HALF)] = encode(jnp.concatenate(both, axis=0), 2)

        z_copy(c).start()

    def stage5(c):
        @pl.when(c == 0)
        def _():
            for copy in par_copies:
                copy.wait()

        z_copy(c).wait_recv()

        @pl.loop(0, WIDE // HALF)
        def _(t):
            sub = pl.ds(pl.multiple_of(t * HALF, HALF), HALF)
            cols = [pl.ds(pl.multiple_of(start_col(c, h) + t * HALF, HALF), HALF) for h in range(2)]
            both = jnp.concatenate([part[rows_of(h, zh, cols[h])] for h in range(2)], axis=0)
            both = decode_add(both, rz[c, :, sub], 2)
            for h in range(2):
                gradient = both[h * 8 : h * 8 + 8]
                first = beta_first * par[1, :, cols[h]] + (1.0 - beta_first) * gradient
                second = beta_second * par[2, :, cols[h]] + (1.0 - beta_second) * gradient * gradient
                fm_ref[:, cols[h]] = first
                sm_ref[:, cols[h]] = second
                update = first / first_correction / (jnp.sqrt(second / second_correction) + epsilon)
                pse[c, h, :, sub] = par[3, :, cols[h]] - (par[0, :, cols[h]] - inner_rate * update)

        m_copy(c).start()

    def stage6(c):
        m_copy(c).wait_recv()
        for i in range(SIDE):
            cols = pl.ds(i * PIECE, PIECE)
            ssum[c, i] = pse[c, k, :, cols] + mrecv[c, :, cols]
        for d in range(1, SIDE):
            l_copy(c, d).start()

    def stage7(c):
        for d in range(1, SIDE):
            l_copy(c, d).wait_recv()
        tot[c, 0] = (ssum[c, q] + lrecv[c, 0]) + (lrecv[c, 1] + lrecv[c, 2])
        for d in range(1, 8):
            b_copy(c, d).start()

    def stage8(c):
        for d in range(1, 8):
            b_copy(c, d).wait_recv()

        @pl.loop(0, 8)
        def _(d):
            src = (rep + 8 - d) % 8
            cols = pl.ds(pl.multiple_of((src % 2) * fh + c * WIDE + (src // 2) * PIECE, PIECE), PIECE)
            average = tot[c, d] / 8.0
            momentum_next = momentum_decay * par[4, :, cols] + average
            mn_ref[:, cols] = momentum_next
            gn_ref[:, cols] = par[3, :, cols] - outer_rate * (average + momentum_decay * momentum_next)

    stages = (stage0, stage1, stage2, stage3, stage4, stage5, stage6, stage7, stage8)

    @pl.loop(0, chunks + len(stages) - 1)
    def _(step):
        for lag, stage in enumerate(stages):
            c = step - lag

            @pl.when((c >= 0) & (c < chunks))
            def _():
                stage(c)

    @pl.loop(0, chunks)
    def _(c):
        for h in range(2):
            for p in range(2):
                for d in range(2):
                    for m in range(2):
                        xy_copy(c, h, p, d, m).wait_send()
        z_copy(c).wait_send()
        m_copy(c).wait_send()
        for d in range(1, SIDE):
            l_copy(c, d).wait_send()
        for d in range(1, 8):
            b_copy(c, d).wait_send()


def shards(
    tok_inputs, tok_grads, inner_params, adam_first, adam_second, global_params, outer_momentum
):
    ff = tok_grads.shape[-1]
    chunks = ff // 2 // WIDE
    out = jax.ShapeDtypeStruct((8, ff), jnp.float32)
    dma = pltpu.SemaphoreType.DMA
    vmem = pl.BlockSpec(memory_space=pltpu.VMEM)
    hbm = pl.BlockSpec(memory_space=pl.ANY)
    f32, b16 = jnp.float32, jnp.bfloat16
    first_moment, second_moment, global_next, momentum_next = pl.pallas_call(
        kernel,
        out_shape=(out,) * 4,
        in_specs=[vmem] + [hbm] * 6,
        out_specs=(vmem,) * 4,
        scratch_shapes=[
            pltpu.VMEM((2, 256, 256), b16),
            pltpu.VMEM((256, ff), b16),
            pltpu.VMEM((5, 8, ff), f32),
            pltpu.VMEM((SIDE, SIDE, 16, ff), f32),
            pltpu.VMEM((chunks, 2, 2, 3, SIDE, 16, HALF), b16),
            pltpu.VMEM((chunks, 2, 2, 3, SIDE, 16, HALF), b16),
            pltpu.VMEM((chunks, 2, 2, 3, 1, 16, HALF), b16),
            pltpu.VMEM((chunks, 2, 2, 3, 1, 16, HALF), b16),
            pltpu.VMEM((chunks, 16, WIDE), b16),
            pltpu.VMEM((chunks, 16, WIDE), b16),
            pltpu.VMEM((chunks, 2, 8, WIDE), f32),
            pltpu.VMEM((chunks, 8, WIDE), f32),
            pltpu.VMEM((chunks, SIDE, 8, PIECE), f32),
            pltpu.VMEM((chunks, SIDE - 1, 8, PIECE), f32),
            pltpu.VMEM((chunks, 8, 8, PIECE), f32),
            dma((chunks, 2)),
            dma((5,)),
            dma((chunks, 16)),
            dma((chunks, 16)),
            dma((chunks,)),
            dma((chunks,)),
            dma((chunks,)),
            dma((chunks,)),
            dma((chunks, SIDE - 1)),
            dma((chunks, SIDE - 1)),
            dma((chunks, 7)),
            dma((chunks, 7)),
        ],
        compiler_params=pltpu.CompilerParams(
            collective_id=0, has_side_effects=True, vmem_limit_bytes=60 * 2**20
        ),
        cost_estimate=pl.CostEstimate(
            flops=2 * 256 * 256 * ff, bytes_accessed=256 * ff * 2 + 9 * 8 * ff * 4, transcendentals=0
        ),
    )(
        tok_inputs[0], tok_grads[0], inner_params[0], adam_first[0], adam_second[0],
        global_params, outer_momentum,
    )
    return (first_moment[None], second_moment[None], global_next, momentum_next)


def solution(mesh):
    rows = P("fsdp", None)
    replicas = P("replica", "fsdp", None)
    return jax.shard_map(
        shards,
        mesh=mesh,
        in_specs=(replicas,) * 5 + (rows,) * 2,
        out_specs=(replicas, replicas, rows, rows),
        check_vma=False,
    )
```

time: 735 us -> 87.8 us (0.12)
  waiting for transfers between devices: 703 us -> 0 us
  Pallas kernels: 0 us -> 79.7 us
  between operations: 14.1 us -> 0.64 us
  matrix products: 10.4 us -> 0 us
    reduce_scatter x1 -> x0, waiting for transfers between devices: 638 us -> none  [shards(): lax.psum_scatter(lax.dot_general(features, upstream, (((0,), (0,)), ((),...]
    pallas_call x0 -> x1, Pallas kernels: none -> 79.7 us  [shards(): pl.pallas_call(kernel, out_shape=(out,) * 4, in_specs=[vmem] + [hbm] * 6,...]
    psum x1 -> x0, waiting for transfers between devices: 65.2 us -> none  [shards(): total = lax.psum(pseudo, 'replica')]
    dot_general x1 -> x0, matrix products: 10.4 us -> none  [shards(): lax.dot_general(features, upstream, (((0,), (0,)), ((), ())), preferred_e...]
  transfers between devices with their start and end apart: 2 -> 0, of which waited for: 2 -> 0; matrix products, arithmetic and copies ran while one was open for 0% -> 0% of each run, Pallas kernels for 0% -> 0%
where the time goes in v1:
time: 87.8 us; the launch traced here: 87.6 us
  Pallas kernels  79.7 us (91%)
  local copies, waits for them, and re-layouts  7.26 us (8%)
    pallas_call x1, Pallas kernels, shards(): pl.pallas_call(kernel, out_shape=(out,) * 4, in_specs=[vmem] + [hbm] * 6,...  79.7 us
    unnamed x4, local copies, waits for them, and re-layouts  7.26 us

profile of v1, /device:TPU:1, one launch (start us, length us, event | category | flops | bytes accessed | tf_op | source)
XLA Modules:
  0.0 87.6 jit_solution(462305146704371047)
XLA Ops:
  0.6 79.7 %shard_map.102 = (f32[8,14336]{1,0:T(8,128)}, f32[8,14336]{1,0:T(8,128)}, f32[8,14336]{1,0:T(8,128)}, f32[8,14336]{1,0:T(8,128)}) custom-call(bf16[256,256]{1,0:T(8,128)(2,1)} %bitcast.13, bf16[256,14336]{1,0:T(8,128)(2,1)} %bitcast.7, f32[8,14336]{1,0:T(8,128)} %bitcast.10, f32[8,14336]{1,0:T(8,128)} %bitcast.11, f32[8,14336]{1,0:T(8,128)} %bitcast.12, ...), custom_call_target="tpu_custom_call" | custom-call | flops 1879048192 | bytes 11468800 | tf_op jit(solution)/shard_map/pallas_call | solution.py:337
  80.3 1.8 %copy.15 = f32[1,8,14336]{2,1,0:T(8,128)} copy(f32[1,8,14336]{2,1,0:T(8,128)} %bitcast.9) | data formatting | bytes 917504
  82.1 1.8 %copy.16 = f32[1,8,14336]{2,1,0:T(8,128)} copy(f32[1,8,14336]{2,1,0:T(8,128)} %bitcast.8) | data formatting | bytes 917504
  83.9 1.8 %copy.17 = f32[8,14336]{1,0:T(8,128)} copy(f32[8,14336]{1,0:T(8,128)} %get-tuple-element.18) | data formatting | bytes 917504
  85.8 1.8 %copy.18 = f32[8,14336]{1,0:T(8,128)} copy(f32[8,14336]{1,0:T(8,128)} %get-tuple-element.19) | data formatting | bytes 917504

commit v2 on v1

v2 whole, which is shorter than its diff:
```python
import functools
import jax
import jax.numpy as jnp
from jax import lax
from jax.experimental import pallas as pl
from jax.experimental.pallas import tpu as pltpu
from jax.sharding import PartitionSpec as P

beta_first = 0.9
beta_second = 0.95
inner_rate = 0.1
outer_rate = 0.7
momentum_decay = 0.9
epsilon = 1e-08
first_correction = 1.0 - 0.9**40
second_correction = 1.0 - 0.95**40

MESH = pl.DeviceIdType.MESH
SIDE = 4
WIDE = 1024
HALF = WIDE // 2
PIECE = WIDE // SIDE
POWER = 7
SCALES = (10, 8, 7)


def encode(value, stage):
    u = value * (2.0 ** SCALES[stage])
    u2 = u * u
    return (u2 * u2 * (u2 * u)).astype(jnp.bfloat16)


def decode_add(total, code, stage):
    y = code.astype(jnp.float32)
    size = jnp.exp2(jnp.log2(jnp.abs(y)) * (1.0 / POWER) - SCALES[stage])
    return jnp.where(y < 0, total - size, total + size)


def moments(first, second, gradient):
    first = beta_first * first + (1.0 - beta_first) * gradient
    second = beta_second * second + (1.0 - beta_second) * gradient * gradient
    return first, second


def sync_kernel(
    feat_ref, g_hbm, p_hbm, a1_hbm, a2_hbm, w_hbm,
    grad_ref, total_ref,
    feat_t, g_ref, par, part, s1a, s1b, r1a, r1b, s2a, s2b, r2a, r2b, sz, rz, pse, lrecv, tot,
    g_sem, par_sem, xy_send, xy_recv, z_send, z_recv, l_send, l_recv, b_send, b_recv,
):
    ff = g_ref.shape[1]
    fh = ff // 2
    chunks = fh // WIDE
    rep = lax.axis_index("replica")
    fs = lax.axis_index("fsdp")
    pos = (fs // 8, (fs // 2) % SIDE)
    zh = fs % 2
    zpeer = (rep, fs + 1 - 2 * zh)

    def ring(axis, step):
        y, x = pos
        if axis == 0:
            y = (y + step) % SIDE
        else:
            x = (x + step) % SIDE
        return (rep, y * 8 + x * 2 + zh)

    rings = [[ring(axis, step) for step in (1, SIDE - 1)] for axis in range(2)]
    near = [[(pos[axis] + step) % SIDE for step in range(SIDE)] for axis in range(2)]
    others = [(rep + d) % 8 for d in range(1, 8)]

    def start_col(c, h):
        return pl.multiple_of(h * fh + c * WIDE, WIDE)

    def g_copy(c, h):
        cols = pl.ds(start_col(c, h), WIDE)
        return pltpu.make_async_copy(g_hbm.at[:, cols], g_ref.at[:, cols], g_sem.at[c, h])

    par_copies = [
        pltpu.make_async_copy(src, par.at[i], par_sem.at[i])
        for i, src in enumerate((p_hbm, a1_hbm, a2_hbm, w_hbm))
    ]
    for h in range(2):
        g_copy(0, h).start()

    barrier = pltpu.get_barrier_semaphore()
    peers = rings[0] + rings[1] + [zpeer] + [(other, fs) for other in others]
    for peer in peers:
        pl.semaphore_signal(barrier, inc=1, device_id=peer, device_id_type=MESH)

    @pl.loop(1, chunks)
    def _(c):
        for h in range(2):
            g_copy(c, h).start()

    for copy in par_copies:
        copy.start()

    feat_t[0] = feat_ref[...].astype(jnp.float32).T.astype(jnp.bfloat16)
    for y in range(SIDE):
        for x in range(SIDE):
            feat_t[1, pl.ds((x * SIDE + y) * 16, 16), :] = feat_t[0, pl.ds((y * SIDE + x) * 16, 16), :]

    sends = ((s1a, s1b), (s2a, s2b))
    recvs = ((r1a, r1b), (r2a, r2b))

    def xy_start(c, p, m):
        for h in range(2):
            for d in range(2):
                pltpu.make_async_remote_copy(
                    src_ref=sends[p][m].at[c, h, d],
                    dst_ref=recvs[p][m].at[c, h, d],
                    send_sem=xy_send.at[2 * p + m],
                    recv_sem=xy_recv.at[c, 2 * p + m],
                    device_id=rings[(h + p) % 2][d],
                    device_id_type=MESH,
                ).start()

    def arrived(ref, sem):
        pltpu.make_async_copy(ref, ref, sem).wait()

    def z_copy(c):
        return pltpu.make_async_remote_copy(
            src_ref=sz.at[c], dst_ref=rz.at[c], send_sem=z_send.at[0], recv_sem=z_recv.at[c],
            device_id=zpeer, device_id_type=MESH,
        )

    def l_start(c):
        for i, other in enumerate(others):
            pltpu.make_async_remote_copy(
                src_ref=pse.at[c, other], dst_ref=lrecv.at[c, i],
                send_sem=l_send.at[0], recv_sem=l_recv.at[c],
                device_id=(other, fs), device_id_type=MESH,
            ).start()

    def b_start(c):
        for i, other in enumerate(others):
            pltpu.make_async_remote_copy(
                src_ref=tot.at[c, 0], dst_ref=tot.at[c, i + 1],
                send_sem=b_send.at[0], recv_sem=b_recv.at[c],
                device_id=(other, fs), device_id_type=MESH,
            ).start()

    def places(c, h, p):
        right = pl.ds(start_col(c, h), HALF)
        left = pl.ds(pl.multiple_of(start_col(c, h) + HALF, HALF), HALF)

        def at(dest, i, cols):
            return (dest, i, slice(None), cols) if p == 0 else (pos[h], dest, slice(None), cols)

        return near[(h + p) % 2], right, left, at

    def over_blocks(p, body):
        if p == 0:
            pl.loop(0, SIDE)(body)
        else:
            body(0)

    def first_sends(c, h, p):
        send = sends[p][0]
        j, right, left, at = places(c, h, p)

        def body(i):
            send[c, h, 0, 0, i] = encode(part[at(j[2], i, right)], p)
            send[c, h, 0, 1, i] = encode(part[at(j[1], i, left)], p)
            send[c, h, 1, 0, i] = encode(part[at(j[2], i, left)], p)
            send[c, h, 1, 1, i] = encode(part[at(j[3], i, right)], p)

        over_blocks(p, body)

    def second_sends(c, h, p):
        send, recv = sends[p][1], recvs[p][0]
        j, right, left, at = places(c, h, p)

        def body(i):
            send[c, h, 0, i] = encode(decode_add(part[at(j[1], i, right)], recv[c, h, 0, 0, i], p), p)
            send[c, h, 1, i] = encode(decode_add(part[at(j[3], i, left)], recv[c, h, 1, 0, i], p), p)

        over_blocks(p, body)

    def collect(c, h, p):
        near_recv, far_recv = recvs[p]
        j, right, left, at = places(c, h, p)

        def body(i):
            part[at(j[0], i, right)] = decode_add(
                decode_add(part[at(j[0], i, right)], far_recv[c, h, 0, i], p), near_recv[c, h, 1, 1, i], p
            )
            part[at(j[0], i, left)] = decode_add(
                decode_add(part[at(j[0], i, left)], near_recv[c, h, 0, 1, i], p), far_recv[c, h, 1, i], p
            )

        over_blocks(p, body)

    def multiply(c, h):
        g_copy(c, h).wait()

        @pl.loop(0, WIDE // 256)
        def _(t):
            cols = pl.ds(pl.multiple_of(start_col(c, h) + t * 256, 256), 256)
            part[:, :, :, cols] = jnp.dot(
                feat_t[h], g_ref[:, cols], preferred_element_type=jnp.float32
            ).reshape(SIDE, SIDE, 16, 256)

    def rows_of(h, whose, cols):
        return (pos[h], pos[1 - h], pl.ds(pl.multiple_of(whose * 8, 8), 8), cols)

    def stage0(c):
        for h in range(2):
            multiply(c, h)
            first_sends(c, h, 0)

        @pl.when(c == 0)
        def _():
            pl.semaphore_wait(barrier, len(peers))

        xy_start(c, 0, 0)

    def second_stage(c, p):
        arrived(recvs[p][0].at[c], xy_recv.at[c, 2 * p])
        for h in range(2):
            second_sends(c, h, p)
        xy_start(c, p, 1)

    def stage1(c):
        second_stage(c, 0)

    def stage2(c):
        arrived(r1b.at[c], xy_recv.at[c, 1])
        for h in range(2):
            collect(c, h, 0)
            first_sends(c, h, 1)
        xy_start(c, 1, 0)

    def stage3(c):
        second_stage(c, 1)

    def stage4(c):
        arrived(r2b.at[c], xy_recv.at[c, 3])
        for h in range(2):
            collect(c, h, 1)

        @pl.loop(0, WIDE // HALF)
        def _(t):
            both = [
                part[rows_of(h, 1 - zh, pl.ds(pl.multiple_of(start_col(c, h) + t * HALF, HALF), HALF))]
                for h in range(2)
            ]
            sz[c, :, pl.ds(pl.multiple_of(t * HALF, HALF), HALF)] = encode(jnp.concatenate(both, axis=0), 2)

        z_copy(c).start()

    def stage5(c):
        @pl.when(c == 0)
        def _():
            for copy in par_copies:
                copy.wait()

        z_copy(c).wait_recv()

        @pl.loop(0, SIDE)
        def _(t):
            sub = pl.ds(pl.multiple_of(t * PIECE, PIECE), PIECE)
            cols = [pl.ds(pl.multiple_of(start_col(c, h) + t * PIECE, PIECE), PIECE) for h in range(2)]
            both = jnp.concatenate([part[rows_of(h, zh, cols[h])] for h in range(2)], axis=0)
            both = decode_add(both, rz[c, :, sub], 2)
            for h in range(2):
                gradient = both[h * 8 : h * 8 + 8]
                grad_ref[:, cols[h]] = gradient
                first, second = moments(par[1, :, cols[h]], par[2, :, cols[h]], gradient)
                update = first / first_correction / (jnp.sqrt(second / second_correction) + epsilon)
                pse[c, 2 * t + h] = par[3, :, cols[h]] - (par[0, :, cols[h]] - inner_rate * update)

        l_start(c)

    def stage6(c):
        arrived(lrecv.at[c], l_recv.at[c])
        total = pse[c, rep]
        for i in range(7):
            total += lrecv[c, i]
        tot[c, 0] = total
        b_start(c)

    def stage7(c):
        arrived(tot.at[c, pl.ds(1, 7)], b_recv.at[c])

        @pl.loop(0, 8)
        def _(d):
            src = (rep + 8 - d) % 8
            cols = pl.ds(pl.multiple_of((src % 2) * fh + c * WIDE + (src // 2) * PIECE, PIECE), PIECE)
            total_ref[:, cols] = tot[c, d]

    stages = (stage0, stage1, stage2, stage3, stage4, stage5, stage6, stage7)

    @pl.loop(0, chunks + len(stages) - 1)
    def _(step):
        for lag, stage in enumerate(stages):
            c = step - lag

            @pl.when((c >= 0) & (c < chunks))
            def _():
                stage(c)

    for ref, sem in zip((s1a, s1b, s2a, s2b), range(4)):
        arrived(ref, xy_send.at[sem])
    arrived(sz, z_send.at[0])
    arrived(lrecv, l_send.at[0])
    arrived(lrecv, b_send.at[0])


def outer_kernel(grad_ref, total_ref, a1_ref, a2_ref, w_ref, m_ref, fm_ref, sm_ref, gn_ref, mn_ref):
    fm_ref[...], sm_ref[...] = moments(a1_ref[...], a2_ref[...], grad_ref[...])
    average = total_ref[...] / 8.0
    momentum_next = momentum_decay * m_ref[...] + average
    mn_ref[...] = momentum_next
    gn_ref[...] = w_ref[...] - outer_rate * (average + momentum_decay * momentum_next)


def shards(
    tok_inputs, tok_grads, inner_params, adam_first, adam_second, global_params, outer_momentum
):
    ff = tok_grads.shape[-1]
    chunks = ff // 2 // WIDE
    out = jax.ShapeDtypeStruct((8, ff), jnp.float32)
    dma = pltpu.SemaphoreType.DMA
    vmem = pl.BlockSpec(memory_space=pltpu.VMEM)
    hbm = pl.BlockSpec(memory_space=pl.ANY)
    f32, b16 = jnp.float32, jnp.bfloat16
    buffers = [
        pltpu.VMEM((chunks, 2, 2) + slots + (blocks, 16, HALF), b16)
        for blocks in (SIDE, 1)
        for _ in range(2)
        for slots in ((2,), ())
    ]
    gradient, total = pl.pallas_call(
        sync_kernel,
        out_shape=(out,) * 2,
        in_specs=[vmem] + [hbm] * 5,
        out_specs=(vmem,) * 2,
        scratch_shapes=[
            pltpu.VMEM((2, 256, 256), b16),
            pltpu.VMEM((256, ff), b16),
            pltpu.VMEM((4, 8, ff), f32),
            pltpu.VMEM((SIDE, SIDE, 16, ff), f32),
            *buffers,
            pltpu.VMEM((chunks, 16, WIDE), b16),
            pltpu.VMEM((chunks, 16, WIDE), b16),
            pltpu.VMEM((chunks, 8, 8, PIECE), f32),
            pltpu.VMEM((chunks, 7, 8, PIECE), f32),
            pltpu.VMEM((chunks, 8, 8, PIECE), f32),
            dma((chunks, 2)),
            dma((4,)),
            dma((4,)),
            dma((chunks, 4)),
            dma((1,)),
            dma((chunks,)),
            dma((1,)),
            dma((chunks,)),
            dma((1,)),
            dma((chunks,)),
        ],
        compiler_params=pltpu.CompilerParams(
            collective_id=0, has_side_effects=True, vmem_limit_bytes=56 * 2**20
        ),
        cost_estimate=pl.CostEstimate(
            flops=2 * 256 * 256 * ff, bytes_accessed=256 * ff * 2 + 6 * 8 * ff * 4, transcendentals=0
        ),
    )(tok_inputs[0], tok_grads[0], inner_params[0], adam_first[0], adam_second[0], global_params)
    first_moment, second_moment, global_next, momentum_next = pl.pallas_call(
        outer_kernel,
        out_shape=(out,) * 4,
        in_specs=[vmem] * 6,
        out_specs=(vmem,) * 4,
    )(gradient, total, adam_first[0], adam_second[0], global_params, outer_momentum)
    return (first_moment[None], second_moment[None], global_next, momentum_next)


def solution(mesh):
    rows = P("fsdp", None)
    replicas = P("replica", "fsdp", None)
    return jax.shard_map(
        shards,
        mesh=mesh,
        in_specs=(replicas,) * 5 + (rows,) * 2,
        out_specs=(replicas, replicas, rows, rows),
        check_vma=False,
    )
```

time: 87.8 us -> 78.4 us (0.89)
  local copies, waits for them, and re-layouts: 7.26 us -> 0 us
  Pallas kernels: 79.7 us -> 77.7 us
    unnamed x4 -> x0, local copies, waits for them, and re-layouts: 7.26 us -> none
    pallas_call x1 -> x2, Pallas kernels: 79.7 us -> 77.7 us  [the longest x1 74.6 us: shards(): pl.pallas_call(sync_kernel, out_shape=(out,) * 2, in_specs=[vmem] + [hbm]...]
where the time goes in v2:
time: 78.4 us; the launch traced here: 78.3 us
  Pallas kernels  77.7 us (99%)
    pallas_call x1, Pallas kernels, shards(): pl.pallas_call(sync_kernel, out_shape=(out,) * 2, in_specs=[vmem] + [hbm]...  74.6 us
    pallas_call x1, Pallas kernels, shards(): pl.pallas_call(outer_kernel, out_shape=(out,) * 4, in_specs=[vmem] * 6, o...  3.02 us

profile of v2, /device:TPU:1, one launch (start us, length us, event | category | flops | bytes accessed | tf_op | source)
XLA Modules:
  0.0 78.3 jit_solution(17947298801822118281)
XLA Ops:
  0.6 74.6 %shard_map.102 = (f32[8,14336]{1,0:T(8,128)}, f32[8,14336]{1,0:T(8,128)}) custom-call(bf16[256,256]{1,0:T(8,128)(2,1)} %bitcast.13, bf16[256,14336]{1,0:T(8,128)(2,1)} %bitcast.7, f32[8,14336]{1,0:T(8,128)} %bitcast.12, f32[8,14336]{1,0:T(8,128)} %bitcast.8, f32[8,14336]{1,0:T(8,128)} %bitcast.10, f32[8,14336]{1,0:T(8,128)} %w_ref.1), custom_call_target="tpu_custom_call" | custom-call | flops 1879048192 | bytes 10092544 | tf_op jit(solution)/shard_map/pallas_call | solution.py:335
  75.3 3.0 %shard_map.103 = (f32[8,14336]{1,0:T(8,128)}, f32[8,14336]{1,0:T(8,128)}, f32[8,14336]{1,0:T(8,128)}, f32[8,14336]{1,0:T(8,128)}) custom-call(f32[8,14336]{1,0:T(8,128)} %get-tuple-element.10.grad_ref, f32[8,14336]{1,0:T(8,128)} %get-tuple-element.11.total_ref, f32[8,14336]{1,0:T(8,128)} %bitcast.9, f32[8,14336]{1,0:T(8,128)} %bitcast.11, f32[8,14336]{1,0:T(8,128)} %w_ref.1, ...), custom_call_target="tpu_custom_call" | custom-call | tf_op jit(solution)/shard_map/pallas_call | solution.py:369

commit v3 on v2

--- a/solution.py
+++ b/solution.py
@@ -17,10 +17,11 @@
 
 MESH = pl.DeviceIdType.MESH
 SIDE = 4
-WIDE = 1024
+WIDE = 512
 HALF = WIDE // 2
 PIECE = WIDE // SIDE
 POWER = 7
+LAGS = (0, 2, 4, 6, 8, 11, 14)
 SCALES = (10, 8, 7)
 
 
@@ -44,8 +45,8 @@
 
 def sync_kernel(
     feat_ref, g_hbm, p_hbm, a1_hbm, a2_hbm, w_hbm,
-    grad_ref, total_ref,
-    feat_t, g_ref, par, part, s1a, s1b, r1a, r1b, s2a, s2b, r2a, r2b, sz, rz, pse, lrecv, tot,
+    grad_ref, tot,
+    feat_t, g_ref, par, part, s1a, s1b, r1a, r1b, s2a, s2b, r2a, r2b, sz, rz, pse, lrecv,
     g_sem, par_sem, xy_send, xy_recv, z_send, z_recv, l_send, l_recv, b_send, b_recv,
 ):
     ff = g_ref.shape[1]
@@ -136,8 +137,8 @@
     def b_start(c):
         for i, other in enumerate(others):
             pltpu.make_async_remote_copy(
-                src_ref=tot.at[c, 0], dst_ref=tot.at[c, i + 1],
-                send_sem=b_send.at[0], recv_sem=b_recv.at[c],
+                src_ref=tot.at[c, rep], dst_ref=tot.at[c, rep],
+                send_sem=b_send.at[0], recv_sem=b_recv.at[0],
                 device_id=(other, fs), device_id_type=MESH,
             ).start()
 
@@ -278,23 +279,14 @@
         total = pse[c, rep]
         for i in range(7):
             total += lrecv[c, i]
-        tot[c, 0] = total
+        tot[c, rep] = total
         b_start(c)
 
-    def stage7(c):
-        arrived(tot.at[c, pl.ds(1, 7)], b_recv.at[c])
-
-        @pl.loop(0, 8)
-        def _(d):
-            src = (rep + 8 - d) % 8
-            cols = pl.ds(pl.multiple_of((src % 2) * fh + c * WIDE + (src // 2) * PIECE, PIECE), PIECE)
-            total_ref[:, cols] = tot[c, d]
-
-    stages = (stage0, stage1, stage2, stage3, stage4, stage5, stage6, stage7)
-
-    @pl.loop(0, chunks + len(stages) - 1)
+    stages = (stage0, stage1, stage2, stage3, stage4, stage5, stage6)
+
+    @pl.loop(0, chunks + LAGS[-1])
     def _(step):
-        for lag, stage in enumerate(stages):
+        for lag, stage in zip(LAGS, stages):
             c = step - lag
 
             @pl.when((c >= 0) & (c < chunks))
@@ -306,14 +298,20 @@
     arrived(sz, z_send.at[0])
     arrived(lrecv, l_send.at[0])
     arrived(lrecv, b_send.at[0])
-
-
-def outer_kernel(grad_ref, total_ref, a1_ref, a2_ref, w_ref, m_ref, fm_ref, sm_ref, gn_ref, mn_ref):
+    arrived(lrecv, b_recv.at[0])
+
+
+def outer_kernel(grad_ref, tot_ref, a1_ref, a2_ref, w_ref, m_ref, fm_ref, sm_ref, gn_ref, mn_ref):
     fm_ref[...], sm_ref[...] = moments(a1_ref[...], a2_ref[...], grad_ref[...])
-    average = total_ref[...] / 8.0
-    momentum_next = momentum_decay * m_ref[...] + average
-    mn_ref[...] = momentum_next
-    gn_ref[...] = w_ref[...] - outer_rate * (average + momentum_decay * momentum_next)
+    chunks, owners, _, piece = tot_ref.shape
+    for c in range(chunks):
+        for owner in range(owners):
+            start = (owner % 2) * chunks * WIDE + c * WIDE + (owner // 2) * piece
+            cols = pl.ds(start, piece)
+            average = tot_ref[c, owner] / 8.0
+            momentum_next = momentum_decay * m_ref[:, cols] + average
+            mn_ref[:, cols] = momentum_next
+            gn_ref[:, cols] = w_ref[:, cols] - outer_rate * (average + momentum_decay * momentum_next)
 
 
 def shards(
@@ -334,7 +332,7 @@
     ]
     gradient, total = pl.pallas_call(
         sync_kernel,
-        out_shape=(out,) * 2,
+        out_shape=(out, jax.ShapeDtypeStruct((chunks, 8, 8, PIECE), f32)),
         in_specs=[vmem] + [hbm] * 5,
         out_specs=(vmem,) * 2,
         scratch_shapes=[
@@ -347,7 +345,6 @@
             pltpu.VMEM((chunks, 16, WIDE), b16),
             pltpu.VMEM((chunks, 8, 8, PIECE), f32),
             pltpu.VMEM((chunks, 7, 8, PIECE), f32),
-            pltpu.VMEM((chunks, 8, 8, PIECE), f32),
             dma((chunks, 2)),
             dma((4,)),
             dma((4,)),
@@ -357,7 +354,7 @@
             dma((1,)),
             dma((chunks,)),
             dma((1,)),
-            dma((chunks,)),
+            dma((1,)),
         ],
         compiler_params=pltpu.CompilerParams(
             collective_id=0, has_side_effects=True, vmem_limit_bytes=56 * 2**20

time: 78.4 us -> 77.7 us (level)
  Pallas kernels: 77.7 us -> 76.9 us
where the time goes in v3:
time: 77.7 us; the launch traced here: 77.6 us
  Pallas kernels  76.9 us (99%)
    pallas_call x1, Pallas kernels, shards(): pl.pallas_call(sync_kernel, out_shape=(out, jax.ShapeDtypeStruct((chunks,...  73.9 us
    pallas_call x1, Pallas kernels, shards(): pl.pallas_call(outer_kernel, out_shape=(out,) * 4, in_specs=[vmem] * 6, o...  3.03 us

profile of v3, /device:TPU:1, one launch (start us, length us, event | category | flops | bytes accessed | tf_op | source)
XLA Modules:
  0.0 77.6 jit_solution(8639473283617050852)
XLA Ops:
  0.6 73.9 %shard_map.102 = (f32[8,14336]{1,0:T(8,128)}, f32[14,8,8,128]{3,2,1,0:T(8,128)}) custom-call(bf16[256,256]{1,0:T(8,128)(2,1)} %bitcast.13, bf16[256,14336]{1,0:T(8,128)(2,1)} %bitcast.7, f32[8,14336]{1,0:T(8,128)} %bitcast.12, f32[8,14336]{1,0:T(8,128)} %bitcast.8, f32[8,14336]{1,0:T(8,128)} %bitcast.10, f32[8,14336]{1,0:T(8,128)} %w_ref.1), custom_call_target="tpu_custom_call" | custom-call | flops 1879048192 | bytes 10092544 | tf_op jit(solution)/shard_map/pallas_call | solution.py:333
  74.5 3.0 %shard_map.103 = (f32[8,14336]{1,0:T(8,128)}, f32[8,14336]{1,0:T(8,128)}, f32[8,14336]{1,0:T(8,128)}, f32[8,14336]{1,0:T(8,128)}) custom-call(f32[8,14336]{1,0:T(8,128)} %get-tuple-element.10.grad_ref, f32[14,8,8,128]{3,2,1,0:T(8,128)} %get-tuple-element.11.tot_ref, f32[8,14336]{1,0:T(8,128)} %bitcast.9, f32[8,14336]{1,0:T(8,128)} %bitcast.11, ...), custom_call_target="tpu_custom_call" | custom-call | tf_op jit(solution)/shard_map/pallas_call | solution.py:366

commit v4 on v3

--- a/solution.py
+++ b/solution.py
@@ -286,7 +286,8 @@
 
     @pl.loop(0, chunks + LAGS[-1])
     def _(step):
-        for lag, stage in zip(LAGS, stages):
+        for n in (0, 6, 5, 1, 2, 3, 4):
+            lag, stage = LAGS[n], stages[n]
             c = step - lag
 
             @pl.when((c >= 0) & (c < chunks))
@@ -303,12 +304,11 @@
 
 def outer_kernel(grad_ref, tot_ref, a1_ref, a2_ref, w_ref, m_ref, fm_ref, sm_ref, gn_ref, mn_ref):
     fm_ref[...], sm_ref[...] = moments(a1_ref[...], a2_ref[...], grad_ref[...])
-    chunks, owners, _, piece = tot_ref.shape
+    chunks, quarters, _, _, piece = tot_ref.shape
     for c in range(chunks):
-        for owner in range(owners):
-            start = (owner % 2) * chunks * WIDE + c * WIDE + (owner // 2) * piece
-            cols = pl.ds(start, piece)
-            average = tot_ref[c, owner] / 8.0
+        for quarter in range(quarters):
+            cols = pl.ds(c * WIDE + quarter * piece, piece)
+            average = tot_ref[c, quarter, 0] / 8.0
             momentum_next = momentum_decay * m_ref[:, cols] + average
             mn_ref[:, cols] = momentum_next
             gn_ref[:, cols] = w_ref[:, cols] - outer_rate * (average + momentum_decay * momentum_next)
@@ -323,6 +323,7 @@
     dma = pltpu.SemaphoreType.DMA
     vmem = pl.BlockSpec(memory_space=pltpu.VMEM)
     hbm = pl.BlockSpec(memory_space=pl.ANY)
+    half = pl.BlockSpec((8, ff // 2), lambda h: (0, h))
     f32, b16 = jnp.float32, jnp.bfloat16
     buffers = [
         pltpu.VMEM((chunks, 2, 2) + slots + (blocks, 16, HALF), b16)
@@ -366,9 +367,10 @@
     first_moment, second_moment, global_next, momentum_next = pl.pallas_call(
         outer_kernel,
         out_shape=(out,) * 4,
-        in_specs=[vmem] * 6,
-        out_specs=(vmem,) * 4,
-    )(gradient, total, adam_first[0], adam_second[0], global_params, outer_momentum)
+        grid=(2,),
+        in_specs=[half, pl.BlockSpec((chunks, SIDE, 1, 8, PIECE), lambda h: (0, 0, h, 0, 0))] + [half] * 4,
+        out_specs=(half,) * 4,
+    )(gradient, total.reshape(chunks, SIDE, 2, 8, PIECE), adam_first[0], adam_second[0], global_params, outer_momentum)
     return (first_moment[None], second_moment[None], global_next, momentum_next)
 
 

time: 77.7 us -> 77.3 us (level)
  no operation moved by 1% of the time
where the time goes in v4:
time: 77.3 us; the launch traced here: 77.2 us
  Pallas kernels  76.6 us (99%)
    pallas_call x1, Pallas kernels, shards(): pl.pallas_call(sync_kernel, out_shape=(out, jax.ShapeDtypeStruct((chunks,...  73.7 us
    pallas_call x1, Pallas kernels, shards(): pl.pallas_call(outer_kernel, out_shape=(out,) * 4, grid=(2,), in_specs=[h...  2.88 us

profile of v4, /device:TPU:1, one launch (start us, length us, event | category | flops | bytes accessed | tf_op | source)
XLA Modules:
  0.0 77.2 jit_solution(9127412477514921300)
XLA Ops:
  0.6 73.7 %shard_map.102 = (f32[8,14336]{1,0:T(8,128)}, f32[14,8,8,128]{3,2,1,0:T(8,128)}) custom-call(bf16[256,256]{1,0:T(8,128)(2,1)} %bitcast.15, bf16[256,14336]{1,0:T(8,128)(2,1)} %bitcast.8, f32[8,14336]{1,0:T(8,128)} %bitcast.13, f32[8,14336]{1,0:T(8,128)} %bitcast.9, f32[8,14336]{1,0:T(8,128)} %bitcast.11, f32[8,14336]{1,0:T(8,128)} %w_ref.1), custom_call_target="tpu_custom_call" | custom-call | flops 1879048192 | bytes 10092544 | tf_op jit(solution)/shard_map/pallas_call | solution.py:334
  74.3 2.9 %shard_map.103 = (f32[8,14336]{1,0:T(8,128)}, f32[8,14336]{1,0:T(8,128)}, f32[8,14336]{1,0:T(8,128)}, f32[8,14336]{1,0:T(8,128)}) custom-call(f32[8,14336]{1,0:T(8,128)} %get-tuple-element.10.grad_ref, f32[14,4,2,8,128]{4,3,2,1,0:T(8,128)} %bitcast.14, f32[8,14336]{1,0:T(8,128)} %bitcast.10, f32[8,14336]{1,0:T(8,128)} %bitcast.12, f32[8,14336]{1,0:T(8,128)} %w_ref.1, ...), custom_call_target="tpu_custom_call" | custom-call | tf_op jit(solution)/shard_map/pallas_call | solution.py:367
